TPU v7x, 128 devices: a whole 4x4x4 slice. The times are simulated.
128 devices in a mesh: section: 8 (over x, y_lo), expert: 16 (over y_hi, z, core).
Axes of the slice: x: 4, y: 4 (y_hi: 2, y_lo: 2; y = y_hi * 2 + y_lo), z: 4, core: 2. Of those that a mesh axis runs over, the one named last changes fastest.
Arguments:
- x_fwd: bfloat16 [8, 1024, 7168], P('section', 'expert'), may hold values from -6 to 6
- routes_fwd: int32 [8, 1024, 2], P('section', 'expert'), may hold values from 0 to 3, as said below
- slots_fwd: int32 [8, 1024, 2], P('section', 'expert'), may hold values from 0 to 35, as said below
- logits_fwd: float32 [8, 1024, 2], P('section', 'expert'), may hold values from -6 to 6
- x_bwd: bfloat16 [8, 1024, 7168], P('section', 'expert'), may hold values from -6 to 6
- cot_bwd: bfloat16 [8, 1024, 7168], P('section', 'expert'), may hold values from -6 to 6
- routes_bwd: int32 [8, 1024, 2], P('section', 'expert'), may hold values from 0 to 3, as said below
- slots_bwd: int32 [8, 1024, 2], P('section', 'expert'), may hold values from 0 to 35, as said below
- logits_bwd: float32 [8, 1024, 2], P('section', 'expert'), may hold values from -6 to 6
- gain: float32 [8, 7168], P('section'), may hold values from 0.5 to 1.5
- w_gate: bfloat16 [8, 7168, 8192], P('section', None, 'expert'), may hold values from -0.0625 to 0.0625
- w_up: bfloat16 [8, 7168, 8192], P('section', None, 'expert'), may hold values from -0.0625 to 0.0625
- w_down: bfloat16 [8, 8192, 7168], P('section', 'expert'), may hold values from -0.125 to 0.125
Outputs:
- fwd_arrived: bfloat16 [8, 1024, 7168], P('section', 'expert')
- grad_arrived: bfloat16 [8, 1024, 7168], P('section', 'expert')
Inputs may be any that keep to these rules, and one draw needn't show every extreme that they name: `routes_fwd`: in each aligned block of 64 rows (the tokens of one index of expert in one layer) a token names 2 different experts, no expert is named by more than 36 tokens, and one expert by exactly 36. `slots_fwd`: an assignment's slot is the number of earlier tokens of its aligned block of 64 rows that name the same expert. `routes_bwd`: as for routes_fwd. `slots_bwd`: as for slots_fwd.
All inputs are finite; a program needn't handle non-finite values.
Results may differ from a plain program's by a relative error of at most 0.0069.
Values may be sent and summed in bfloat16 or wider, within the bound.
A program may use at most 192 MiB of HBM per device.

v0:
```python
import jax
import jax.numpy as jnp
from jax import lax
from jax.sharding import PartitionSpec as P

D = 7168
EXP_WIN = 4
TOPK = 2
CAP = 36


epsilon = 1e-06
route_scale = 2.5


def passed_along(block, axis, distance):
    devices = range(lax.axis_size(axis))
    route = [((i - distance) % len(devices), i) for i in devices]
    return lax.ppermute(block, axis, route)


def normalize(inputs, gain_row):
    widened = inputs.astype(jnp.float32)
    inverse = lax.rsqrt(jnp.mean(widened * widened, axis=-1, keepdims=True) + epsilon)
    normed = (widened * inverse * gain_row[None, :]).astype(jnp.bfloat16)
    return (widened, inverse, normed)


def mixing(logits):
    affinity = jax.nn.sigmoid(logits)
    return route_scale * affinity / jnp.sum(affinity, axis=-1, keepdims=True)


def slot_map(routes, slots):
    columns = (routes * CAP + slots).reshape(-1)
    matches = columns[None, :] == jnp.arange(EXP_WIN * CAP, dtype=jnp.int32)[:, None]
    token_ids = jnp.arange(columns.shape[0], dtype=jnp.int32) // TOPK
    owner = jnp.sum(jnp.where(matches, token_ids[None, :], 0), axis=1)
    filled = jnp.any(matches, axis=1)
    return (matches, owner, filled)


def place(values, owner, filled):
    placed = jnp.where(filled[:, None], values[owner], jnp.zeros((), jnp.bfloat16))
    return placed


def fan_out(placed, group):
    width = placed.shape[-1]
    return jnp.repeat(placed.reshape(EXP_WIN, CAP, width), group, axis=0)


def expert_forward(received, gate_w, up_w, down_w):
    width = received.shape[-1]
    flat_rows = received.reshape(-1, width)
    gate_pre = jnp.dot(flat_rows, gate_w, preferred_element_type=jnp.float32)
    up_pre = jnp.dot(flat_rows, up_w, preferred_element_type=jnp.float32)
    hidden = (jax.nn.silu(gate_pre) * up_pre).astype(jnp.bfloat16)
    partial_value = jnp.dot(hidden, down_w, preferred_element_type=jnp.float32).astype(jnp.bfloat16)
    return partial_value.reshape(received.shape)


def expert_backward(received, cot_received, gate_w, up_w, down_w):
    width = received.shape[-1]
    flat_rows = received.reshape(-1, width)
    cot_flat = cot_received.reshape(-1, width)
    contract = (((1,), (1,)), ((), ()))
    gate_pre = jnp.dot(flat_rows, gate_w, preferred_element_type=jnp.float32)
    up_pre = jnp.dot(flat_rows, up_w, preferred_element_type=jnp.float32)
    sigma = jax.nn.sigmoid(gate_pre)
    d_hidden = lax.dot_general(cot_flat, down_w, contract, preferred_element_type=jnp.float32)
    d_gate = (d_hidden * up_pre * sigma * (1.0 + gate_pre * (1.0 - sigma))).astype(jnp.bfloat16)
    d_up = (d_hidden * gate_pre * sigma).astype(jnp.bfloat16)
    partial_value = lax.dot_general(d_gate, gate_w, contract, preferred_element_type=jnp.float32)
    partial_value = partial_value + lax.dot_general(
        d_up, up_w, contract, preferred_element_type=jnp.float32
    )
    return partial_value.astype(jnp.bfloat16).reshape(received.shape)


def collect(returned, group, routes, slots):
    width = returned.shape[-1]
    summed = jnp.sum(returned.reshape(EXP_WIN, group, CAP, width).astype(jnp.float32), axis=1)
    return summed.reshape(EXP_WIN * CAP, width)[routes * CAP + slots]


def on_device(
    x_fwd,
    routes_fwd,
    slots_fwd,
    logits_fwd,
    x_bwd,
    cot_bwd,
    routes_bwd,
    slots_bwd,
    logits_bwd,
    gain,
    w_gate,
    w_up,
    w_down,
):
    group = lax.axis_size("expert") // EXP_WIN
    gain_row = gain[0]
    gate_w = w_gate[0]
    up_w = w_up[0]
    down_w = w_down[0]
    widened, inverse, normed = normalize(x_fwd[0], gain_row)
    shares = mixing(logits_fwd[0])
    matches, owner, filled = slot_map(routes_fwd[0], slots_fwd[0])
    send_forward = fan_out(place(normed, owner, filled), group)
    back_widened, back_inverse, back_normed = normalize(x_bwd[0], gain_row)
    back_shares = mixing(logits_bwd[0])
    back_matches, back_owner, back_filled = slot_map(routes_bwd[0], slots_bwd[0])
    send_inputs = fan_out(place(back_normed, back_owner, back_filled), group)
    cotangent = cot_bwd[0]
    weight_row = jnp.sum(
        jnp.where(back_matches, back_shares.reshape(-1)[None, :], jnp.zeros((), jnp.float32)),
        axis=1,
    )
    cot_rows = (
        place(cotangent, back_owner, back_filled).astype(jnp.float32) * weight_row[:, None]
    ).astype(jnp.bfloat16)
    send_cot = fan_out(cot_rows, group)
    back_forward = lax.all_to_all(
        expert_forward(
            lax.all_to_all(send_forward, "expert", split_axis=0, concat_axis=0, tiled=True),
            gate_w,
            up_w,
            down_w,
        ),
        "expert",
        split_axis=0,
        concat_axis=0,
        tiled=True,
    )
    back_backward = lax.all_to_all(
        expert_backward(
            lax.all_to_all(send_inputs, "expert", split_axis=0, concat_axis=0, tiled=True),
            lax.all_to_all(send_cot, "expert", split_axis=0, concat_axis=0, tiled=True),
            gate_w,
            up_w,
            down_w,
        ),
        "expert",
        split_axis=0,
        concat_axis=0,
        tiled=True,
    )
    picked = collect(back_forward, group, routes_fwd[0], slots_fwd[0])
    result = (widened + jnp.sum(shares[:, :, None] * picked, axis=1)).astype(jnp.bfloat16)
    d_normed = jnp.sum(collect(back_backward, group, routes_bwd[0], slots_bwd[0]), axis=1)
    scaled = gain_row[None, :] * d_normed
    along = jnp.sum(back_widened * scaled, axis=-1, keepdims=True) / D
    d_inputs = (
        cotangent.astype(jnp.float32)
        + back_inverse * scaled
        - back_widened * back_inverse * back_inverse * back_inverse * along
    )
    d_inputs = d_inputs.astype(jnp.bfloat16)
    arrived = passed_along(result, "section", 1)
    returned = passed_along(d_inputs, "section", -1)
    return (arrived[None], returned[None])


def solution(mesh):
    return jax.shard_map(
        on_device,
        mesh=mesh,
        in_specs=(
            P("section", "expert", None),
            P("section", "expert", None),
            P("section", "expert", None),
            P("section", "expert", None),
            P("section", "expert", None),
            P("section", "expert", None),
            P("section", "expert", None),
            P("section", "expert", None),
            P("section", "expert", None),
            P("section", None),
            P("section", None, "expert"),
            P("section", None, "expert"),
            P("section", "expert", None),
        ),
        out_specs=(P("section", "expert", None), P("section", "expert", None)),
        check_vma=False,
    )
```

profile of v0, /device:TPU:96, one launch (start us, length us, event | category | flops | bytes accessed | tf_op | source)
XLA Modules:
  0.0 946.7 jit_solution(13542609946955489014)
XLA Ops:
  0.6 1.9 fusion.49
  2.8 0.1 div.84
  3.0 0.7 compare_select_fusion.2
  4.2 1.3 compare_select_fusion.3
  5.8 0.2 select_reduce_fusion.1
  5.9 6.4 gather_fusion.2
  12.3 1.8 gather.25
  14.2 0.7 multiply_convert_fusion
  14.9 4.7 broadcast_in_dim.101
  19.6 7.3 all-to-all-start.2
  26.8 0.3 fusion.21
  27.1 0.3 fusion.25
  27.4 0.3 fusion.16
  27.7 3.2 gather_fusion.3
  30.9 1.8 gather.27
  32.7 1.6 broadcast_select_fusion
  34.3 131.0 %all-to-all-done.2 = bf16[16,36,7168]{2,1,0:T(8,128)(2,1)} async-done(((bf16[16,36,7168]{2,1,0:T(8,128)(2,1)}), bf16[16,36,7168]{2,1,0:T(8,128)(2,1)}, u32[]{:S(2)}, u32[]{:S(2)}) %all-to-all-start.2) | async-done | bytes 8257568 | tf_op jit(solution)/shard_map/all_to_all | solution.py:139
  165.3 6.4 broadcast_in_dim.102
  171.7 8.8 all-to-all-start.3
  180.5 9.7 %reshape.286 = bf16[576,7168]{1,0:T(8,128)(2,1)} reshape(bf16[16,36,7168]{2,1,0:T(8,128)(2,1)} %all-to-all-done.2) | data formatting | bytes 16515072 | tf_op jit(solution)/shard_map/reshape | solution.py:66
  190.2 10.9 %fusion = f32[576,512]{1,0:T(8,128)} fusion(bf16[576,7168]{1,0:T(8,128)(2,1)} %reshape.286, bf16[1,512,7168]{2,1,0:T(8,128)(2,1)} %param.25), kind=kOutput, calls=%fused_computation.9 | convolution fusion | flops 4227858432 | bytes 16777216 | tf_op jit(solution)/shard_map/dot_general | solution.py:71
  201.1 117.8 %all-to-all-done.3 = bf16[16,36,7168]{2,1,0:T(8,128)(2,1)} async-done(((bf16[16,36,7168]{2,1,0:T(8,128)(2,1)}), bf16[16,36,7168]{2,1,0:T(8,128)(2,1)}, u32[]{:S(2)}, u32[]{:S(2)}) %all-to-all-start.3) | async-done | bytes 8257568 | tf_op jit(solution)/shard_map/all_to_all | solution.py:138
  318.8 9.9 %reshape.288 = bf16[576,7168]{1,0:T(8,128)(2,1)} reshape(bf16[16,36,7168]{2,1,0:T(8,128)(2,1)} %all-to-all-done.3) | data formatting | bytes 16515072 | tf_op jit(solution)/shard_map/reshape | solution.py:65
  328.7 9.1 fusion.10
  337.8 1.0 copy-done.15
  338.8 7.8 fusion.42
  346.6 8.3 fusion.8
  354.9 13.4 %add_convert_fusion = bf16[576,7168]{1,0:T(8,128)(2,1)} fusion(f32[576,7168]{1,0:T(8,128)} %fusion.8, bf16[1,7168,512]{2,1,0:T(8,128)(2,1)} %param.24, f32[576,512]{1,0:T(8,128)} %fusion, f32[576,512]{1,0:T(8,128)} %copy-done.15), kind=kOutput, calls=%fused_computation.7 | convolution fusion | flops 4237885440 | bytes 34471936 | tf_op jit(solution)/shard_map/dot_general | solution.py:75
  368.3 9.6 %reshape.289 = bf16[16,36,7168]{2,1,0:T(8,128)(2,1)} reshape(bf16[576,7168]{1,0:T(8,128)(2,1)} %add_convert_fusion) | data formatting | bytes 16515072 | tf_op jit(solution)/shard_map/reshape | solution.py:78
  377.9 8.4 all-to-all-start.4
  386.7 138.0 %all-to-all-done.4 = bf16[16,36,7168]{2,1,0:T(8,128)(2,1)} async-done(((bf16[16,36,7168]{2,1,0:T(8,128)(2,1)}), bf16[16,36,7168]{2,1,0:T(8,128)(2,1)}, u32[]{:S(2)}, u32[]{:S(2)}) %all-to-all-start.4) | async-done | bytes 8257568 | tf_op jit(solution)/shard_map/all_to_all | solution.py:136
  524.7 7.9 convert_reduce_fusion
  532.7 3.8 reshape.290
  536.5 7.2 gather_fusion.4
  543.7 5.6 reshape.336
  549.4 6.5 reduce_sum.124
  555.9 0.3 fusion.26
  556.2 0.8 copy-done
  557.0 0.3 copy-done.3
  557.3 0.3 copy-done.5
  557.6 1.8 fusion.20
  559.4 3.2 gather_fusion
  562.6 1.8 gather.22
  564.4 1.6 broadcast_select_fusion.1
  566.0 2.9 broadcast_in_dim.95
  568.9 111.4 %all_to_all.25 = bf16[16,36,7168]{2,1,0:T(8,128)(2,1)} all-to-all(bf16[16,36,7168]{2,1,0:T(8,128)(2,1)S(1)} %bitcast.80), channel_id=1, replica_groups=mesh['section'=8,'expert'=16] {'expert'}, dimensions={0} | all-to-all | bytes 16515072 | tf_op jit(solution)/shard_map/all_to_all | solution.py:126
  680.3 9.8 %reshape.282 = bf16[576,7168]{1,0:T(8,128)(2,1)} reshape(bf16[16,36,7168]{2,1,0:T(8,128)(2,1)} %all_to_all.25) | data formatting | bytes 16515072 | tf_op jit(solution)/shard_map/reshape | solution.py:55
  690.1 9.1 fusion.12
  699.3 4.5 fusion.39
  703.8 9.9 %convolution_convert_fusion = bf16[576,7168]{1,0:T(8,128)(2,1)} fusion(bf16[576,512]{1,0:T(8,128)(2,1)S(1)} %fusion.39, bf16[1,512,7168]{2,1,0:T(8,128)(2,1)} %param.25), kind=kOutput, calls=%fused_computation.8 | convolution fusion | flops 4231987200 | bytes 16187392 | tf_op jit(solution)/shard_map/dot_general | solution.py:59
  713.6 9.6 %reshape.283 = bf16[16,36,7168]{2,1,0:T(8,128)(2,1)} reshape(bf16[576,7168]{1,0:T(8,128)(2,1)} %convolution_convert_fusion) | data formatting | bytes 16515072 | tf_op jit(solution)/shard_map/reshape | solution.py:60
  723.3 6.9 all-to-all-start.1
  730.3 0.1 reshape.309
  730.6 0.2 collective-permute-start.1
  730.7 156.8 %all-to-all-done.1 = bf16[16,36,7168]{2,1,0:T(8,128)(2,1)} async-done(((bf16[16,36,7168]{2,1,0:T(8,128)(2,1)}), bf16[16,36,7168]{2,1,0:T(8,128)(2,1)}, u32[]{:S(2)}, u32[]{:S(2)}) %all-to-all-start.1) | async-done | bytes 8257568 | tf_op jit(solution)/shard_map/all_to_all | solution.py:124
  887.6 7.9 convert_reduce_fusion.1
  895.5 4.1 reshape.284
  899.6 7.2 gather_fusion.1
  906.8 5.5 reshape.308
  912.3 7.2 multiply_reduce_fusion
  919.5 0.2 fusion.24
  919.7 24.6 %collective-permute-done = bf16[64,7168]{1,0:T(8,128)(2,1)S(1)} collective-permute-done((bf16[64,7168]{1,0:T(8,128)(2,1)S(1)}, bf16[64,7168]{1,0:T(8,128)(2,1)S(1)}, u32[]{:S(2)}, u32[]{:S(2)}) %collective-permute-start) | collective-permute-done | bytes 917536 | tf_op jit(solution)/shard_map/ppermute | solution.py:19
  944.4 0.9 copy.35
  945.3 0.9 copy.36
  (69 shorter events, 2.0 us)
Async XLA Ops:
  19.5 7.3 copy-start.4
  19.5 7.6 copy-start.1
  19.5 7.9 copy-start.10
  19.6 145.8 %all-to-all-start.2 = ((bf16[16,36,7168]{2,1,0:T(8,128)(2,1)}), bf16[16,36,7168]{2,1,0:T(8,128)(2,1)}, u32[]{:S(2)}, u32[]{:S(2)}) async-start(bf16[16,36,7168]{2,1,0:T(8,128)(2,1)} %bitcast.78), calls=%async_computation.2 | async-start | bytes 18350080 | tf_op jit(solution)/shard_map/all_to_all | solution.py:139
  171.7 147.1 %all-to-all-start.3 = ((bf16[16,36,7168]{2,1,0:T(8,128)(2,1)}), bf16[16,36,7168]{2,1,0:T(8,128)(2,1)}, u32[]{:S(2)}, u32[]{:S(2)}) async-start(bf16[16,36,7168]{2,1,0:T(8,128)(2,1)} %bitcast.79), calls=%async_computation.3 | async-start | bytes 18350080 | tf_op jit(solution)/shard_map/all_to_all | solution.py:138
  318.8 27.8 %slice-start = ((s8[7340032]{0:T(1024)(128)(4,1)}), s8[3145728]{0:T(1024)(128)(4,1)S(1)}, s32[]{:S(2)}) async-start(s8[7340032]{0:T(1024)(128)(4,1)} %bitcast.81), calls=%async_computation.5 | async-start | bytes 6291456
  328.7 10.1 %copy-start.7 = (bf16[576,7168]{1,0:T(8,128)(2,1)S(1)}, bf16[576,7168]{1,0:T(8,128)(2,1)}, u32[]{:S(2)}) copy-start(bf16[576,7168]{1,0:T(8,128)(2,1)} %reshape.288) | copy-start | bytes 24772612
  328.7 10.1 %copy-start.14 = (f32[576,512]{1,0:T(8,128)S(1)}, f32[576,512]{1,0:T(8,128)}, u32[]{:S(2)}) copy-start(f32[576,512]{1,0:T(8,128)} %fusion) | copy-start | bytes 3538948
  328.7 17.9 %slice-start.1 = ((s8[7340032]{0:T(1024)(128)(4,1)}), s8[4194304]{0:T(1024)(128)(4,1)S(1)}, s32[]{:S(2)}) async-start(s8[7340032]{0:T(1024)(128)(4,1)} %bitcast.81), calls=%async_computation.6 | async-start | bytes 8388608
  337.8 1.0 copy-start.15
  377.9 146.8 %all-to-all-start.4 = ((bf16[16,36,7168]{2,1,0:T(8,128)(2,1)}), bf16[16,36,7168]{2,1,0:T(8,128)(2,1)}, u32[]{:S(2)}, u32[]{:S(2)}) async-start(bf16[16,36,7168]{2,1,0:T(8,128)(2,1)} %reshape.289), calls=%async_computation.4 | async-start | bytes 18350080 | tf_op jit(solution)/shard_map/all_to_all | solution.py:136
  549.4 6.5 copy-start.2
  555.9 1.2 copy-start
  555.9 1.4 copy-start.3
  555.9 1.7 copy-start.5
  680.3 18.9 %slice-start.2 = ((s8[7340032]{0:T(1024)(128)(4,1)}), s8[3145728]{0:T(1024)(128)(4,1)S(1)}, s32[]{:S(2)}) async-start(s8[7340032]{0:T(1024)(128)(4,1)} %bitcast.92), calls=%async_computation.7 | async-start | bytes 6291456
  690.1 9.1 copy-start.8
  690.1 9.1 slice-start.3
  723.3 6.9 copy-start.12
  723.3 7.2 copy-start.11
  723.3 7.2 copy-start.13
  723.3 7.3 copy-start.9
  723.3 164.3 %all-to-all-start.1 = ((bf16[16,36,7168]{2,1,0:T(8,128)(2,1)}), bf16[16,36,7168]{2,1,0:T(8,128)(2,1)}, u32[]{:S(2)}, u32[]{:S(2)}) async-start(bf16[16,36,7168]{2,1,0:T(8,128)(2,1)} %reshape.283), calls=%async_computation.1 | async-start | bytes 18350080 | tf_op jit(solution)/shard_map/all_to_all | solution.py:124
  730.6 189.1 %collective-permute-start.1 = (bf16[64,7168]{1,0:T(8,128)(2,1)S(1)}, bf16[64,7168]{1,0:T(8,128)(2,1)S(1)}, u32[]{:S(2)}, u32[]{:S(2)}) collective-permute-start(bf16[64,7168]{1,0:T(8,128)(2,1)S(1)} %copy-done.9), channel_id=1, source_target_pairs={{16,0},{32,16},{48,32},{64,48},{80,64},{96,80},{112,96},{0,112},{1... | collective-permute-start | bytes 2752520 | tf_op jit(solution)/shard_map/ppermute | solution.py:19
  912.3 7.2 copy-start.6
  919.6 24.7 %collective-permute-start = (bf16[64,7168]{1,0:T(8,128)(2,1)S(1)}, bf16[64,7168]{1,0:T(8,128)(2,1)S(1)}, u32[]{:S(2)}, u32[]{:S(2)}) collective-permute-start(bf16[64,7168]{1,0:T(8,128)(2,1)S(1)} %fusion.24), channel_id=1, source_target_pairs={{112,0},{0,16},{16,32},{32,48},{48,64},{64,80},{80,96},{96,112},{1... | collective-permute-start | bytes 2752520 | tf_op jit(solution)/shard_map/ppermute | solution.py:19
where the time goes:
time: 955 us; the launch traced here: 947 us
  waiting for transfers between devices  568 us (59%)
  local copies, waits for them, and re-layouts  120 us (13%)
  blocking collectives  111 us (12%)
  matrix products  72.8 us (8%)
  other arithmetic  41.1 us (4%)
  starting transfers between devices  31.6 us (3%)
    all_to_all x1, waiting for transfers between devices, on_device(): lax.all_to_all(expert_forward(lax.all_to_all(send_forward, 'expert', spli...  157 us
    all_to_all x1, waiting for transfers between devices, on_device(): lax.all_to_all(expert_backward(lax.all_to_all(send_inputs, 'expert', spli...  138 us
    all_to_all x1, waiting for transfers between devices, on_device(): lax.all_to_all(send_cot, 'expert', split_axis=0, concat_axis=0, tiled=True)  131 us
    all_to_all x1, waiting for transfers between devices, on_device(): lax.all_to_all(send_inputs, 'expert', split_axis=0, concat_axis=0, tiled=...  118 us
    all_to_all x1, blocking collectives, on_device(): lax.all_to_all(send_forward, 'expert', split_axis=0, concat_axis=0, tiled...  111 us
    gather x4, local copies, waits for them, and re-layouts, collect(): return summed.reshape(EXP_WIN * CAP, width)[routes * CAP + slots]  25.5 us
    ppermute x2, waiting for transfers between devices, passed_along(): return lax.ppermute(block, axis, route)  24.6 us
  transfers between devices with their start and end apart: 6, of which 5 were waited for; matrix products, arithmetic and copies ran while one was open for 6% of the time, Pallas kernels for 0%

commit v1 on v0

v1 whole, which is shorter than its diff:
```python
import jax
import jax.numpy as jnp
from jax import lax
from jax.experimental import pallas as pl
from jax.experimental.pallas import tpu as pltpu
from jax.sharding import PartitionSpec as P

D = 7168
EXP_WIN = 4
TOPK = 2
CAP = 36
TOK = 64
HID = 512
PAIR = 4 * CAP
SLOTS = EXP_WIN * PAIR
CH = 896
NK = 4
NKK = 2 * NK

epsilon = 1e-06
route_scale = 2.5
MESH = pl.DeviceIdType.MESH
BF = jnp.bfloat16
F32 = jnp.float32


class Place:
    def __init__(self):
        me = lax.axis_index("expert")
        self.core = lax.rem(me, 2)
        z = lax.rem(me // 2, 4)
        a = me // 8
        b = z // 2
        zl = lax.rem(z, 2)
        self.h = b + zl - 2 * b * zl
        zg = z + 1 - 2 * zl

        def at(a_, z_, c_):
            return a_ * 8 + z_ * 2 + c_

        self.mate = at(a, z, 1 - self.core)
        self.g = at(a, zg, self.core)
        self.gmate = at(a, zg, 1 - self.core)
        self.c = at(a, 3 - z, self.core)
        self.y = at(1 - a, z, self.core)
        self.pairs = (a * 2 + b, a * 2 + 1 - b, (1 - a) * 2 + b, (1 - a) * 2 + 1 - b)
        self.index = self.h * 2 + self.core


class Copies:
    def __init__(self, sems):
        self.sems = sems
        self.used = 0

    def sem(self):
        self.used += 1
        return self.sems.at[self.used - 1]

    def remote(self, src, dst, device, axis="expert"):
        copy = pltpu.make_async_remote_copy(
            src_ref=src,
            dst_ref=dst,
            send_sem=self.sem(),
            recv_sem=self.sem(),
            device_id={axis: device},
            device_id_type=MESH,
        )
        copy.start()
        return copy

    def local(self, src, dst):
        copy = pltpu.make_async_copy(src, dst, self.sem())
        copy.start()
        return copy


def greet(places, others=()):
    barrier = pltpu.get_barrier_semaphore()
    for place in places:
        pl.semaphore_signal(barrier, inc=1, device_id={"expert": place}, device_id_type=MESH)
    for place in others:
        pl.semaphore_signal(barrier, inc=1, device_id={"section": place}, device_id_type=MESH)
    pl.semaphore_wait(barrier, len(places) + len(others))


def rows64(first):
    return pl.ds(pl.multiple_of(first, 64), 64)


def rows128(first):
    return pl.ds(pl.multiple_of(first, 128), 128)


def rows144(pair):
    return pl.ds(pl.multiple_of(pair * PAIR, PAIR), PAIR)


def dispatch_kernel(
    xf, xb, cot, gain, meta, rows, metas_out,
    hbuf, tok, stage, relay, metas, place_m, sems,
):
    at = Place()
    cp = Copies(sems)
    greet((at.mate, at.g, at.gmate, at.c, at.y))
    h, core = at.h, at.core
    half = core * NK
    other = (1 - core) * NK
    mine = metas.at[at.index]
    meta_sends = [cp.remote(meta, mine, d) for d in (at.mate, at.g, at.gmate)]
    metas[at.index] = meta[...]

    my_rows = h * 128 + core * 64
    tok_in = []
    for t, src in enumerate((xf, xb, cot)):
        if t < 2:
            total = jnp.zeros((TOK, 1), F32)
            for kk in range(NKK):
                v = src[:, kk * CH:(kk + 1) * CH].astype(F32)
                total = total + jnp.sum(v * v, axis=-1, keepdims=True)
            inverse = lax.rsqrt(total / D + epsilon)
        for kk in range(NKK):
            v = src[:, kk * CH:(kk + 1) * CH]
            if t < 2:
                v = (v.astype(F32) * inverse * gain[:, kk * CH:(kk + 1) * CH]).astype(BF)
            hbuf[t, kk] = v
        tok_in.append(cp.remote(
            hbuf.at[t, pl.ds(other, NK)], tok.at[t, :, rows64(my_rows), :], at.mate))
        for k in range(NK):
            tok[t, k, rows64(my_rows), :] = hbuf[t, half + k]

    steps = [(t, i) for t in range(3) for i in range(NK)]
    n = len(steps)
    tok_g = {}

    def send_tokens(s):
        if s >= n:
            return
        t, i = steps[s]
        if i == 0:
            tok_in[t].wait_recv()
        q = lax.rem(2 * (1 - h) + i, NK)
        piece = tok.at[t, q, rows128(h * 128), :]
        tok_g[s] = cp.remote(piece, piece, at.g)

    for s in range(3):
        send_tokens(s)

    for m in meta_sends:
        m.wait_recv()
    for fb in range(2):
        for rel in range(4):
            first = at.pairs[rel] * PAIR
            ids = (lax.broadcasted_iota(jnp.int32, (PAIR, 128), 0) + first).astype(F32)
            for hh in range(2):
                m = metas[2 * hh] + metas[2 * hh + 1]
                k0 = m[fb * 8:fb * 8 + 1, :]
                k1 = m[fb * 8 + 1:fb * 8 + 2, :]
                hit = jnp.where(ids == k0, 1.0, 0.0) + jnp.where(ids == k1, 1.0, 0.0)
                place_m[fb, rel, :, hh * 128:(hh + 1) * 128] = hit.astype(BF)
    metas_out[...] = metas[...]

    sent = {}
    moved = {}
    passed = {}
    mate_in = []

    def gather(s):
        t, i = steps[s]
        slot = s % 3
        if s >= 3:
            for key in [k for k in list(sent) if k[0] == s - 3]:
                sent[key].wait_send()
            moved[s - 3].wait()
        tok_g[s].wait_recv()
        q = lax.rem(2 * h + i, NK)
        fb = 0 if t == 0 else 1
        block = tok[t, q]
        order = (3, 2, 1, 0) if i < 2 else (2, 1, 0)
        for rel in order:
            stage[slot, rel] = jnp.dot(
                place_m[fb, rel], block, preferred_element_type=F32).astype(BF)
            src = stage.at[slot, rel]
            target = rows.at[t, half + q, rows144(at.pairs[0]), :]
            if rel == 3:
                sent[s, 3] = cp.remote(src, relay.at[t, i], at.y)
            elif rel == 2:
                sent[s, 2] = cp.remote(src, target, at.y)
            elif rel == 1:
                sent[s, 1] = cp.remote(src, target, at.c)
            else:
                moved[s] = cp.local(src, target)
                sent[s, 0] = cp.remote(src, target, at.mate)
                mate_in.append(sent[s, 0])

    def to_mate(t, chunk, pair):
        piece = rows.at[t, half + chunk, rows144(pair), :]
        copy = cp.remote(piece, piece, at.mate)
        mate_in.append(copy)
        passed[len(passed)] = copy

    def relay_first(s):
        if not 0 <= s < n or steps[s][1] >= 2:
            return
        t, i = steps[s]
        sent[s, 3].wait_recv()
        passed["c", s] = cp.remote(
            relay.at[t, i], rows.at[t, half + 2 * h + i, rows144(at.pairs[2]), :], at.c)

    def relay_second(s):
        if not 0 <= s < n or steps[s][1] >= 2:
            return
        t, i = steps[s]
        passed["c", s].wait_recv()
        piece = rows.at[t, half + 2 * h + i, rows144(at.pairs[3]), :]
        passed["g", s] = cp.remote(piece, piece, at.g)
        to_mate(t, 2 * h + i, at.pairs[3])

    def relay_last(s):
        if not 0 <= s < n or steps[s][1] >= 2:
            return
        t, i = steps[s]
        passed["g", s].wait_recv()
        to_mate(t, 2 * (1 - h) + i, at.pairs[3])

    def pass_on(s):
        if not 0 <= s < n:
            return
        t, i = steps[s]
        q = lax.rem(2 * h + i, NK)
        sent[s, 2].wait_recv()
        to_mate(t, q, at.pairs[2])
        sent[s, 1].wait_recv()
        to_mate(t, q, at.pairs[1])

    for s in range(n + 3):
        send_tokens(s + 3)
        if s < n:
            gather(s)
        relay_first(s - 1)
        relay_second(s - 2)
        pass_on(s - 1)
        relay_last(s - 3)

    for m in meta_sends + tok_in + list(tok_g.values()) + list(passed.values()):
        m.wait_send()
    for (s, rel), m in sent.items():
        if s >= n - 3:
            m.wait_send()
    for s in range(n - 3, n):
        moved[s].wait()
    for m in mate_in:
        m.wait_recv()


def dispatch(x_fwd, x_bwd, cot, gain, meta):
    vmem = pl.BlockSpec(memory_space=pltpu.VMEM)
    return pl.pallas_call(
        dispatch_kernel,
        out_shape=(
            jax.ShapeDtypeStruct((3, NKK, SLOTS, CH), BF),
            jax.ShapeDtypeStruct((4, 16, 128), F32),
        ),
        in_specs=[vmem] * 5,
        out_specs=(pl.BlockSpec(memory_space=pl.ANY), vmem),
        scratch_shapes=[
            pltpu.VMEM((3, NKK, TOK, CH), BF),
            pltpu.VMEM((3, NK, 256, CH), BF),
            pltpu.VMEM((3, 4, PAIR, CH), BF),
            pltpu.VMEM((3, 2, PAIR, CH), BF),
            pltpu.VMEM((4, 16, 128), F32),
            pltpu.VMEM((2, 4, PAIR, 256), BF),
            pltpu.SemaphoreType.DMA((260,)),
        ],
        compiler_params=pltpu.CompilerParams(
            collective_id=1, has_side_effects=True, vmem_limit_bytes=60 * 2 ** 20),
        name="dispatch",
    )(x_fwd, x_bwd, cot, gain, meta)


def forward_hidden_kernel(rows, wg, wu, act, gate, up):
    k = pl.program_id(0)

    @pl.when(k == 0)
    def _():
        gate[...] = jnp.zeros_like(gate)
        up[...] = jnp.zeros_like(up)

    r = rows[0, 0]
    gate[...] += jnp.dot(r, wg[...], preferred_element_type=F32)
    up[...] += jnp.dot(r, wu[...], preferred_element_type=F32)

    @pl.when(k == NKK - 1)
    def _():
        g = gate[...]
        act[...] = (g * jax.nn.sigmoid(g) * up[...]).astype(BF)


def forward_out_kernel(act, wd, out):
    out[0] = jnp.dot(act[...], wd[...], preferred_element_type=F32).astype(BF)


CONTRACT = (((1,), (1,)), ((), ()))


def backward_hidden_kernel(rows, cots, wg, wu, wd, dg, du, gate, up, dact):
    k = pl.program_id(0)

    @pl.when(k == 0)
    def _():
        gate[...] = jnp.zeros_like(gate)
        up[...] = jnp.zeros_like(up)
        dact[...] = jnp.zeros_like(dact)

    r = rows[0, 0]
    gate[...] += jnp.dot(r, wg[...], preferred_element_type=F32)
    up[...] += jnp.dot(r, wu[...], preferred_element_type=F32)
    dact[...] += lax.dot_general(cots[0, 0], wd[...], CONTRACT, preferred_element_type=F32)

    @pl.when(k == NKK - 1)
    def _():
        g = gate[...]
        s = jax.nn.sigmoid(g)
        d = dact[...]
        dg[...] = (d * up[...] * s * (1.0 + g * (1.0 - s))).astype(BF)
        du[...] = (d * g * s).astype(BF)


def backward_out_kernel(dg, du, wg, wu, out):
    v = lax.dot_general(dg[...], wg[...], CONTRACT, preferred_element_type=F32)
    v = v + lax.dot_general(du[...], wu[...], CONTRACT, preferred_element_type=F32)
    out[0] = v.astype(BF)


def experts(rows, wg, wu, wd):
    def rows_of(t):
        return pl.BlockSpec((1, 1, SLOTS, CH), lambda k: (t, k, 0, 0))

    tall = pl.BlockSpec((CH, HID), lambda k: (k, 0))
    wide = pl.BlockSpec((HID, CH), lambda k: (0, k))
    hidden = pl.BlockSpec((SLOTS, HID), lambda k: (0, 0))
    out = pl.BlockSpec((1, SLOTS, CH), lambda k: (k, 0, 0))
    hidden_shape = jax.ShapeDtypeStruct((SLOTS, HID), BF)
    out_shape = jax.ShapeDtypeStruct((NKK, SLOTS, CH), BF)
    acc = pltpu.VMEM((SLOTS, HID), F32)
    params = pltpu.CompilerParams(vmem_limit_bytes=60 * 2 ** 20)
    act = pl.pallas_call(
        forward_hidden_kernel, grid=(NKK,), out_shape=hidden_shape,
        in_specs=[rows_of(0), tall, tall], out_specs=hidden,
        scratch_shapes=[acc, acc], compiler_params=params, name="forward_hidden",
    )(rows, wg, wu)
    forward = pl.pallas_call(
        forward_out_kernel, grid=(NKK,), out_shape=out_shape,
        in_specs=[hidden, wide], out_specs=out, compiler_params=params, name="forward_out",
    )(act, wd)
    dg, du = pl.pallas_call(
        backward_hidden_kernel, grid=(NKK,), out_shape=(hidden_shape, hidden_shape),
        in_specs=[rows_of(1), rows_of(2), tall, tall, wide], out_specs=(hidden, hidden),
        scratch_shapes=[acc, acc, acc], compiler_params=params, name="backward_hidden",
    )(rows, rows, wg, wu, wd)
    backward = pl.pallas_call(
        backward_out_kernel, grid=(NKK,), out_shape=out_shape,
        in_specs=[hidden, hidden, tall, tall], out_specs=out, compiler_params=params,
        name="backward_out",
    )(dg, du, wg, wu)
    return forward, backward


def return_kernel(
    of, ob, xf, xb, cot, gain, metas, yf_out, dx_out,
    own, part, total, from_y, from_c, from_g, pass_y, from_yc, comb_own, comb_out, comb_in,
    spread, acc, result, meta_t, weights, sems,
):
    at = Place()
    cp = Copies(sems)
    me_s = lax.axis_index("section")
    up_s = lax.rem(me_s + 1, 8)
    down_s = lax.rem(me_s + 7, 8)
    greet((at.mate, at.g, at.c, at.y), (up_s, down_s))
    h, core = at.h, at.core
    half = core * NK
    other = (1 - core) * NK
    steps = [(t, i) for t in range(2) for i in range(NK)]
    n = len(steps)

    def chunk(i):
        return lax.rem(2 * (1 - h) + i, NK)

    outs = (of, ob)
    parts = []
    for s, (t, i) in enumerate(steps):
        q = chunk(i)
        parts.append(cp.remote(outs[t].at[other + q], part.at[t, q], at.mate))

    loads = {}

    def load(s):
        if s < n:
            t, i = steps[s]
            loads[s] = cp.local(outs[t].at[half + chunk(i)], own.at[s % 2])

    load(0)
    load(1)

    meta_t[...] = jnp.zeros_like(meta_t)
    for w in range(2):
        hh = h if w == 0 else 1 - h
        meta_t[0:16, :] = metas[2 * hh] + metas[2 * hh + 1]
        m = jnp.transpose(meta_t[...])
        for fb in range(2):
            for rel in range(4):
                first = at.pairs[rel] * PAIR
                ids = (lax.broadcasted_iota(jnp.int32, (128, PAIR), 1) + first).astype(F32)
                c = fb * 8
                v = jnp.where(ids == m[:, c:c + 1], m[:, c + 2:c + 3], 0.0)
                v = v + jnp.where(ids == m[:, c + 1:c + 2], m[:, c + 3:c + 4], 0.0)
                high = v.astype(BF)
                weights[fb, rel, 0, w * 128:(w + 1) * 128, :] = high
                weights[fb, rel, 1, w * 128:(w + 1) * 128, :] = (v - high.astype(F32)).astype(BF)

    sent = {}

    def add_up(s):
        t, i = steps[s]
        q = chunk(i)
        loads[s].wait()
        parts[s].wait_recv()
        total[t, q] = (own[s % 2].astype(F32) + part[t, q].astype(F32)).astype(BF)
        load(s + 2)

        def piece(rel):
            return total.at[t, q, rows144(at.pairs[rel]), :]

        if i < 2:
            sent["g", s] = cp.remote(piece(3), from_g.at[t, i], at.g)
        else:
            sent["g", s - 2].wait_recv()
            pass_y[t, i - 2] = (
                total[t, q, rows144(at.pairs[3]), :].astype(F32) + from_g[t, i - 2].astype(F32)
            ).astype(BF)
            sent["yg", s] = cp.remote(pass_y.at[t, i - 2], from_yc.at[t, i - 2, 0], at.c)
        sent["y", s] = cp.remote(piece(2), from_y.at[t, q], at.y)
        sent["c", s] = cp.remote(piece(1), from_c.at[t, q], at.c)

    def relay(s):
        if not 0 <= s < n or steps[s][1] < 2:
            return
        t, i = steps[s]
        sent["yg", s].wait_recv()
        sent["ygy", s] = cp.remote(from_yc.at[t, i - 2, 0], from_yc.at[t, i - 2, 1], at.y)

    def combine(s):
        if not 0 <= s < n:
            return
        t, i = steps[s]
        q = chunk(i)
        sent["y", s].wait_recv()
        sent["c", s].wait_recv()
        terms = [
            (0, total[t, q, rows144(at.pairs[0]), :]),
            (1, from_c[t, q]),
            (2, from_y[t, q]),
        ]
        if i >= 2:
            sent["ygy", s].wait_recv()
            terms.append((3, from_yc[t, i - 2, 1]))
        v = jnp.zeros((256, CH), F32)
        for rel, r in terms:
            v = v + jnp.dot(weights[t, rel, 0], r, preferred_element_type=F32)
            v = v + jnp.dot(weights[t, rel, 1], r, preferred_element_type=F32)
        comb_own[t, q] = v[0:128]
        comb_out[t, q] = v[128:256].astype(BF)
        sent["u", s] = cp.remote(comb_out.at[t, q], comb_in.at[t, q], at.g)

    def finish(s):
        t, i = steps[s]
        q = chunk(i)
        sent["u", t * NK + (i + 2) % NK].wait_recv()
        v = comb_own[t, q] + comb_in[t, q].astype(F32)
        spread[t, q, 0] = v[0:64]
        spread[t, q, 1] = v[64:128]
        sent["d", s] = cp.remote(spread.at[t, q, 1 - core], acc.at[t, half + q], at.mate)
        acc[t, half + q] = spread[t, q, core]

    def finalize(t):
        for i in range(NK):
            sent["d", t * NK + i].wait_recv()
        if t == 0:
            for kk in range(NKK):
                cols = slice(kk * CH, (kk + 1) * CH)
                result[0, :, cols] = (xf[:, cols].astype(F32) + acc[0, kk]).astype(BF)
            sent["s", 0] = cp.remote(result.at[0], yf_out, up_s, "section")
        else:
            total_sq = jnp.zeros((TOK, 1), F32)
            along = jnp.zeros((TOK, 1), F32)
            for kk in range(NKK):
                cols = slice(kk * CH, (kk + 1) * CH)
                x = xb[:, cols].astype(F32)
                total_sq = total_sq + jnp.sum(x * x, axis=-1, keepdims=True)
                along = along + jnp.sum(x * (gain[:, cols] * acc[1, kk]), axis=-1, keepdims=True)
            inverse = lax.rsqrt(total_sq / D + epsilon)
            factor = inverse * inverse * inverse * (along / D)
            for kk in range(NKK):
                cols = slice(kk * CH, (kk + 1) * CH)
                x = xb[:, cols].astype(F32)
                v = cot[:, cols].astype(F32) + inverse * (gain[:, cols] * acc[1, kk]) - x * factor
                result[1, :, cols] = v.astype(BF)
            sent["s", 1] = cp.remote(result.at[1], dx_out, down_s, "section")

    for s in range(n + 4):
        if s < n:
            add_up(s)
        relay(s - 1)
        combine(s - 2)
        if s - 2 == NK - 1:
            for i in range(NK):
                finish(i)
        if s - 3 == NK - 1:
            finalize(0)
        if s - 2 == n - 1:
            for i in range(NK):
                finish(NK + i)
    finalize(1)
    for m in parts:
        m.wait_send()
    for m in sent.values():
        m.wait_send()
    for t in range(2):
        sent["s", t].wait_recv()


def give_back(forward, backward, x_fwd, x_bwd, cot, gain, metas):
    vmem = pl.BlockSpec(memory_space=pltpu.VMEM)
    hbm = pl.BlockSpec(memory_space=pl.ANY)
    return pl.pallas_call(
        return_kernel,
        out_shape=(jax.ShapeDtypeStruct((TOK, D), BF),) * 2,
        in_specs=[hbm, hbm] + [vmem] * 5,
        out_specs=(hbm, hbm),
        scratch_shapes=[
            pltpu.VMEM((2, SLOTS, CH), BF),
            pltpu.VMEM((2, NK, SLOTS, CH), BF),
            pltpu.VMEM((2, NK, SLOTS, CH), BF),
            pltpu.VMEM((2, NK, PAIR, CH), BF),
            pltpu.VMEM((2, NK, PAIR, CH), BF),
            pltpu.VMEM((2, 2, PAIR, CH), BF),
            pltpu.VMEM((2, 2, PAIR, CH), BF),
            pltpu.VMEM((2, 2, 2, PAIR, CH), BF),
            pltpu.VMEM((2, NK, 128, CH), F32),
            pltpu.VMEM((2, NK, 128, CH), BF),
            pltpu.VMEM((2, NK, 128, CH), BF),
            pltpu.VMEM((2, NK, 2, TOK, CH), F32),
            pltpu.VMEM((2, NKK, TOK, CH), F32),
            pltpu.VMEM((2, TOK, D), BF),
            pltpu.VMEM((128, 128), F32),
            pltpu.VMEM((2, 4, 2, 256, PAIR), BF),
            pltpu.SemaphoreType.DMA((140,)),
        ],
        compiler_params=pltpu.CompilerParams(
            collective_id=2, has_side_effects=True, vmem_limit_bytes=60 * 2 ** 20),
        name="give_back",
    )(forward, backward, x_fwd, x_bwd, cot, gain, metas)


def describe(routes, slots, logits):
    me = lax.axis_index("expert")
    core = lax.rem(me, 2)
    z = lax.rem(me // 2, 4)
    b = z // 2
    zl = lax.rem(z, 2)
    index = (b + zl - 2 * b * zl) * 2 + core
    affinity = jax.nn.sigmoid(logits)
    share = route_scale * affinity / jnp.sum(affinity, axis=-1, keepdims=True)
    key = (routes * PAIR + index * CAP + slots).astype(F32)
    table = jnp.concatenate([key.T, share.T, jnp.zeros((4, TOK), F32)], axis=0)
    zeros = jnp.zeros_like(table)
    return jnp.where(
        core == 0,
        jnp.concatenate([table, zeros], axis=1),
        jnp.concatenate([zeros, table], axis=1),
    )


def on_device(
    x_fwd, routes_fwd, slots_fwd, logits_fwd,
    x_bwd, cot_bwd, routes_bwd, slots_bwd, logits_bwd,
    gain, w_gate, w_up, w_down,
):
    meta = jnp.concatenate([
        describe(routes_fwd[0], slots_fwd[0], logits_fwd[0]),
        describe(routes_bwd[0], slots_bwd[0], logits_bwd[0]),
    ], axis=0)
    rows, metas = dispatch(x_fwd[0], x_bwd[0], cot_bwd[0], gain, meta)
    forward, backward = experts(rows, w_gate[0], w_up[0], w_down[0])
    arrived, returned = give_back(
        forward, backward, x_fwd[0], x_bwd[0], cot_bwd[0], gain, metas)
    return (arrived[None], returned[None])


def solution(mesh):
    return jax.shard_map(
        on_device,
        mesh=mesh,
        in_specs=(
            P("section", "expert", None),
            P("section", "expert", None),
            P("section", "expert", None),
            P("section", "expert", None),
            P("section", "expert", None),
            P("section", "expert", None),
            P("section", "expert", None),
            P("section", "expert", None),
            P("section", "expert", None),
            P("section", None),
            P("section", None, "expert"),
            P("section", None, "expert"),
            P("section", "expert", None),
        ),
        out_specs=(P("section", "expert", None), P("section", "expert", None)),
        check_vma=False,
    )
```

time: 955 us -> 333 us (0.35)
  waiting for transfers between devices: 568 us -> 0 us
  Pallas kernels: 0 us -> 319 us
  local copies, waits for them, and re-layouts: 120 us -> 4.4 us
  blocking collectives: 111 us -> 0 us
  matrix products: 72.8 us -> 0 us
  other arithmetic: 41.1 us -> 2.29 us
  starting transfers between devices: 31.6 us -> 0 us
    all_to_all x4 -> x0, waiting for transfers between devices: 544 us -> none  [the longest x1 157 us: on_device(): lax.all_to_all(expert_forward(lax.all_to_all(send_forward, 'expert', spli...]
    pallas_call x0 -> x6, Pallas kernels: none -> 319 us  [the longest x1 131 us: give_back(): pl.pallas_call(return_kernel, out_shape=(jax.ShapeDtypeStruct((TOK, D), B...]
    all_to_all x1 -> x0, blocking collectives: 111 us -> none  [on_device(): lax.all_to_all(send_forward, 'expert', split_axis=0, concat_axis=0, tiled...]
    dot_general x8 -> x0, matrix products: 72.8 us -> none  [the longest x1 13.4 us: expert_backward(): lax.dot_general(d_up, up_w, contract, preferred_element_type=jnp.float32)]
    reshape x7 -> x0, local copies, waits for them, and re-layouts: 56.6 us -> none  [the longest x1 9.91 us: expert_backward(): flat_rows = received.reshape(-1, width)]
    gather x10 -> x0, local copies, waits for them, and re-layouts: 43.6 us -> none  [the longest x4 25.5 us: collect(): return summed.reshape(EXP_WIN * CAP, width)[routes * CAP + slots]]
    reduce_sum x10 -> x1, other arithmetic: 32.6 us -> 0.72 us  [describe(): share = route_scale * affinity / jnp.sum(affinity, axis=-1, keepdims=True)]
    all_to_all x4 -> x0, starting transfers between devices: 31.4 us -> none  [the longest x1 8.77 us: on_device(): lax.all_to_all(send_inputs, 'expert', split_axis=0, concat_axis=0, tiled=...]
  transfers between devices with their start and end apart: 6 -> 0, of which waited for: 5 -> 0; matrix products, arithmetic and copies ran while one was open for 6% -> 0% of each run, Pallas kernels for 0% -> 0%
where the time goes in v1:
time: 333 us; the launch traced here: 327 us
  Pallas kernels  319 us (96%)
  local copies, waits for them, and re-layouts  4.4 us (1%)
    pallas_call x1, Pallas kernels, give_back(): pl.pallas_call(return_kernel, out_shape=(jax.ShapeDtypeStruct((TOK, D), B...  131 us
    pallas_call x1, Pallas kernels, dispatch(): pl.pallas_call(dispatch_kernel, out_shape=(jax.ShapeDtypeStruct((3, NKK,...  124 us
    pallas_call x1, Pallas kernels, experts(): pl.pallas_call(backward_hidden_kernel, grid=(NKK,), out_shape=(hidden_sha...  21.4 us
    pallas_call x1, Pallas kernels, experts(): pl.pallas_call(backward_out_kernel, grid=(NKK,), out_shape=out_shape, in_...  15.7 us
    pallas_call x1, Pallas kernels, experts(): pl.pallas_call(forward_hidden_kernel, grid=(NKK,), out_shape=hidden_shape...  15.6 us
    pallas_call x1, Pallas kernels, experts(): pl.pallas_call(forward_out_kernel, grid=(NKK,), out_shape=out_shape, in_s...  11.1 us

profile of v1, /device:TPU:96, one launch (start us, length us, event | category | flops | bytes accessed | tf_op | source)
XLA Modules:
  0.0 326.5 jit_solution(10013013724000770173)
XLA Ops:
  0.7 0.1 pad.11.clone
  0.8 0.7 convert_bitcast_fusion
  1.5 0.7 fusion.2
  2.2 0.1 maximum_maximum_fusion
  2.3 0.1 pad_select_fusion.1
  2.4 0.1 pad_select_fusion
  2.5 0.6 pad_maximum_fusion.meta
  3.1 123.7 %dispatch.1 = (bf16[3,8,576,896]{3,2,1,0:T(8,128)(2,1)}, f32[4,16,128]{2,1,0:T(8,128)}) custom-call(bf16[64,7168]{1,0:T(8,128)(2,1)} %bitcast.36, bf16[64,7168]{1,0:T(8,128)(2,1)} %bitcast.38, bf16[64,7168]{1,0:T(8,128)(2,1)} %bitcast.40, f32[1,7168]{1,0:T(1,128)} %gain.3, f32[16,128]{1,0:T(8,128)} %pad_maximum_fusion.meta), custom_call_target="tpu_custom_call" | custom-call | tf_op jit(solution)/shard_map/dispatch/pallas_call | solution.py:257
  126.8 15.6 %forward_hidden.1.act = bf16[576,512]{1,0:T(8,128)(2,1)} custom-call(bf16[3,8,576,896]{3,2,1,0:T(8,128)(2,1)} %get-tuple-element.8.rows.cots, bf16[7168,512]{1,0:T(8,128)(2,1)} %bitcast.28, bf16[7168,512]{1,0:T(8,128)(2,1)} %bitcast.31), custom_call_target="tpu_custom_call" | custom-call | tf_op jit(solution)/shard_map/forward_hidden/pallas_call | solution.py:346
  142.5 21.4 %backward_hidden.1 = (bf16[576,512]{1,0:T(8,128)(2,1)}, bf16[576,512]{1,0:T(8,128)(2,1)}) custom-call(bf16[3,8,576,896]{3,2,1,0:T(8,128)(2,1)} %get-tuple-element.8.rows.cots, bf16[3,8,576,896]{3,2,1,0:T(8,128)(2,1)} %get-tuple-element.8.rows.cots, bf16[7168,512]{1,0:T(8,128)(2,1)} %bitcast.29, bf16[7168,512]{1,0:T(8,128)(2,1)} %bitcast.32, ...), custom_call_target="tpu_custom_call" | custom-call | tf_op jit(solution)/shard_map/backward_hidden/pallas_call | solution.py:355
  163.9 15.7 %backward_out.1.ob = bf16[8,576,896]{2,1,0:T(8,128)(2,1)} custom-call(bf16[576,512]{1,0:T(8,128)(2,1)} %get-tuple-element.9.dg, bf16[576,512]{1,0:T(8,128)(2,1)} %get-tuple-element.10.du, bf16[7168,512]{1,0:T(8,128)(2,1)} %bitcast.30, bf16[7168,512]{1,0:T(8,128)(2,1)} %bitcast.33), custom_call_target="tpu_custom_call" | custom-call | tf_op jit(solution)/shard_map/backward_out/pallas_call | solution.py:360
  179.6 11.1 %forward_out.1.of = bf16[8,576,896]{2,1,0:T(8,128)(2,1)} custom-call(bf16[576,512]{1,0:T(8,128)(2,1)} %forward_hidden.1.act, bf16[512,7168]{1,0:T(8,128)(2,1)} %bitcast.35), custom_call_target="tpu_custom_call" | custom-call | tf_op jit(solution)/shard_map/forward_out/pallas_call | solution.py:351
  190.7 131.5 %give_back.1 = (bf16[64,7168]{1,0:T(8,128)(2,1)}, bf16[64,7168]{1,0:T(8,128)(2,1)}) custom-call(bf16[8,576,896]{2,1,0:T(8,128)(2,1)} %forward_out.1.of, bf16[8,576,896]{2,1,0:T(8,128)(2,1)} %backward_out.1.ob, bf16[64,7168]{1,0:T(8,128)(2,1)} %bitcast.37, bf16[64,7168]{1,0:T(8,128)(2,1)} %bitcast.39, bf16[64,7168]{1,0:T(8,128)(2,1)} %bitcast.41, ...), custom_call_target="tpu_custom_call" | custom-call | tf_op jit(solution)/shard_map/give_back/pallas_call | solution.py:534
  322.2 2.2 copy.17
  324.4 2.2 copy.18
  (3 shorter events, 0.0 us)
